TPU v7x, 128 devices: a whole 4x4x4 slice. The times are simulated.
128 devices in a mesh: stn: 8 (over x_lo, y), src: 16 (over z, x_hi, core).
Axes of the slice: x: 4 (x_hi: 2, x_lo: 2; x = x_hi * 2 + x_lo), y: 4, z: 4, core: 2. Of those that a mesh axis runs over, the one named last changes fastest.
Arguments:
- beam_jones: bfloat16 [8, 512, 16384], P(None, 'stn', 'src'), may hold values from -3 to 3
- source_lm: float32 [2, 16384], P(None, 'src'), may hold values from -0.3 to 0.3
- source_flux: float32 [16384], P('src'), may hold values from 0.3 to 3
- live_counts: int32 [16], P('src'), may hold values from 1 to 1024, 9216 in all
- station_uvw: float32 [3, 512], replicated, may hold values from -400 to 400
- chan_scale: float32 [4], replicated, may hold values from 0.9 to 1.1
- block_pairs: int32 [136, 2], P('stn'), may hold values from 0 to 15, as said below
Outputs:
- visibility: float32 [136, 32768], P('stn', 'src')
Inputs may be any that keep to these rules, and one draw needn't show every extreme that they name: `block_pairs`: each row holds two station blocks i <= j; every such pair of the 16 blocks appears exactly once. `live_counts`: some shard is full (1024 live); the counts sum to 9216.
All inputs are finite; a program needn't handle non-finite values.
Results may differ from a plain program's by a relative error of at most 0.00081.
Values may be sent and summed in bfloat16 or wider, within the bound.
No kernel may reach another device: no remote copies, remote signals or barrier semaphores. Data moves between devices by JAX's collectives and lax.ppermute only.
A program may use at most 128 MiB of HBM per device.

v0:
```python
import math

import jax
import jax.numpy as jnp
from jax import lax
from jax.sharding import PartitionSpec as P

NBLK = 16
SRC_BLOCK = 256


def beam_field(jones_slab, sky_lm, weights, station_uvw, chan_scale):
    dir_l = sky_lm[0]
    dir_m = sky_lm[1]
    w_depth = jnp.sqrt(1.0 - dir_l * dir_l - dir_m * dir_m) - 1.0
    geometry = (
        station_uvw[0][:, None] * dir_l[None, :]
        + station_uvw[1][:, None] * dir_m[None, :]
        + station_uvw[2][:, None] * w_depth[None, :]
    )
    phases = 2.0 * math.pi * chan_scale[:, None, None] * geometry[None]
    cosine = jnp.cos(phases)[:, :, None, None, :]
    sine_part = jnp.sin(phases)[:, :, None, None, :]
    components = jones_slab.astype(jnp.float32).reshape(
        2, 2, 2, jones_slab.shape[1], jones_slab.shape[2]
    )
    real_jones = jnp.transpose(components[0], (2, 0, 1, 3))[None]
    imag_jones = jnp.transpose(components[1], (2, 0, 1, 3))[None]
    amplitude = jnp.sqrt(weights)
    field_re = (real_jones * cosine + imag_jones * sine_part) * amplitude
    field_im = (imag_jones * cosine - real_jones * sine_part) * amplitude
    out_shape = (chan_scale.shape[0], 2 * jones_slab.shape[1], 2 * jones_slab.shape[2])
    return (
        field_re.reshape(out_shape).astype(jnp.bfloat16),
        field_im.reshape(out_shape).astype(jnp.bfloat16),
    )


def gather_beams(jones_part):
    return lax.all_gather(jones_part, "stn", axis=1, tiled=True)


def body(beam_jones, source_lm, source_flux, live_counts, station_uvw, chan_scale, block_pairs):
    shards = lax.axis_size("src")
    slot_count = beam_jones.shape[2]
    stations = station_uvw.shape[1]
    slot_index = jnp.arange(slot_count, dtype=jnp.int32)
    live_flag = (slot_index < live_counts[0]).astype(jnp.float32)
    weights = source_flux * live_flag / math.sqrt(slot_count * shards)
    beams = gather_beams(beam_jones)
    live_total = live_counts[0]
    channels = chan_scale.shape[0]
    block_rows = 2 * stations // NBLK
    local_pairs = block_pairs.shape[0]
    left_block = block_pairs[:, 0]
    right_block = block_pairs[:, 1]
    turns = (live_total + SRC_BLOCK - 1) // SRC_BLOCK

    def one_turn(turn_index, running):
        start_at = (turn_index * SRC_BLOCK).astype(jnp.int32)
        slab = lax.dynamic_slice_in_dim(beams, start_at, SRC_BLOCK, 2)
        sky_part = lax.dynamic_slice_in_dim(source_lm, start_at, SRC_BLOCK, 1)
        share = lax.dynamic_slice_in_dim(weights, start_at, SRC_BLOCK, 0)
        field_re, field_im = beam_field(slab, sky_part, share, station_uvw, chan_scale)
        field_re = field_re.reshape(channels, NBLK, block_rows, 2 * SRC_BLOCK)
        field_im = field_im.reshape(channels, NBLK, block_rows, 2 * SRC_BLOCK)
        left_re = jnp.take(field_re, left_block, axis=1)
        left_im = jnp.take(field_im, left_block, axis=1)
        right_re = jnp.take(field_re, right_block, axis=1)
        right_im = jnp.take(field_im, right_block, axis=1)

        def gram(left, right):
            return jnp.einsum("cnxk,cnyk->ncxy", left, right, preferred_element_type=jnp.float32)

        real_part = gram(left_re, right_re) + gram(left_im, right_im)
        imag_part = gram(left_im, right_re) - gram(left_re, right_im)
        return running + jnp.stack([real_part, imag_part], axis=2)

    start_zero = jnp.zeros((local_pairs, channels, 2, block_rows, block_rows), jnp.float32)
    totals = lax.fori_loop(0, turns, one_turn, start_zero)
    return lax.psum_scatter(totals.reshape(local_pairs, -1), "src", scatter_dimension=1, tiled=True)


def solution(mesh):
    placed = (P(None, "stn", "src"), P(None, "src"), P("src"), P("src"), P(), P(), P("stn", None))
    return jax.shard_map(
        body, mesh=mesh, in_specs=placed, out_specs=P("stn", "src"), check_vma=False
    )
```

profile of v0, /device:TPU:0, one launch (start us, length us, event | category | flops | bytes accessed | tf_op | source)
XLA Modules:
  0.0 663.2 jit_solution(3483576097691024730)
XLA Ops:
  11.6 92.4 %all-gather.2.cloned.1.call-done = bf16[8,512,1024]{2,0,1:T(8,128)(2,1)} async-done(((bf16[8,64,1024]{2,0,1:T(8,128)(2,1)}), bf16[8,512,1024]{2,0,1:T(8,128)(2,1)}) %all-gather.2.cloned.1.call-update) | async-done | bytes 8388624 | tf_op jit(solution)/shard_map/all_gather | solution.py:40
  106.7 465.1 %while.12 = (s32[]{:T(128)}, f32[17,4,2,64,64]{4,3,1,0,2:T(8,128)}, s32[]{:T(128)}, bf16[8,512,1024]{2,0,1:T(8,128)(2,1)}, f32[4]{0:T(128)S(1)}, /*index=5*/f32[...) while((s32[]{:T(128)}, f32[17,4,2,64,64]{4,3,1,0,2:T(8,128)}, ...), condition=%wide.region_1.3_spmd, body=%wide.region_0.2_spmd.sunk | while | flops 1183550976 | bytes 254327120 | solution.py:80
  107.8 7.3 %multiply_cosine_fusion.2 = (f32[4,512,256]{2,1,0:T(8,128)S(1)}, f32[4,512,256]{2,1,0:T(8,128)S(1)}) fusion(f32[512,256]{1,0:T(8,128)S(1)} %multiply_add_fusion.2, f32[4]{0:T(128)S(1)} %broadcast_multiply_fusion.2), kind=kLoop, calls=%fused_computation.24.clone.1 | loop fusion | flops 524288 | bytes 4718608 | tf_op jit(solution)/shard_map/while/body/cos | solution.py:22
  115.1 4.3 mul.315
  119.4 11.5 %mul.316 = f32[4,16,64,512]{3,2,1,0:T(8,128)} reshape(f32[4,512,2,2,256]{4,3,2,1,0:T(2,128)} %mul.315) | data formatting | bytes 16777216 | tf_op jit(solution)/shard_map/while/body/mul | solution.py:30
  130.9 4.1 mul.317
  135.0 11.5 %mul.318 = f32[4,16,64,512]{3,2,1,0:T(8,128)} reshape(f32[4,512,2,2,256]{4,3,2,1,0:T(2,128)} %mul.317) | data formatting | bytes 16777216 | tf_op jit(solution)/shard_map/while/body/mul | solution.py:30
  151.1 2.9 squeeze.32
  156.7 2.9 squeeze.33
  162.5 11.5 %multiply_convert_fusion.3 = (bf16[4,16,64,512]{3,2,1,0:T(8,128)(2,1)}, bf16[4,16,64,512]{3,2,1,0:T(8,128)(2,1)}) fusion(f32[4,16,64,512]{3,2,1,0:T(8,128)} %mul.316, f32[4,16,64,512]{3,2,1,0:T(8,128)} %mul.318, f32[512]{0:T(512)S(1)} %bitcast.103, f32[16,64,512]{2,1,0:T(8,128)} %mul.319, f32[16,64,512]{2,1,0:T(8,128)} %mul.320), kind=kLoop, calls=%fused_computation.4.clone.1 | loop fusion | flops 20971520 | bytes 29362176 | tf_op jit(solution)/shard_map/while/body/convert_element_type | solution.py:35
  174.0 6.0 gather_fusion.1
  180.0 6.0 gather_fusion.3
  186.0 6.5 fusion.49
  192.4 6.1 gather_fusion
  198.5 6.1 gather_fusion.2
  204.6 5.8 add_bitcast_fusion.2
  213.7 3.9 subtract_bitcast_fusion.2
  217.6 5.4 maximum_add_fusion.2
  224.1 7.3 %multiply_cosine_fusion.2 = (f32[4,512,256]{2,1,0:T(8,128)S(1)}, f32[4,512,256]{2,1,0:T(8,128)S(1)}) fusion(f32[512,256]{1,0:T(8,128)S(1)} %multiply_add_fusion.2, f32[4]{0:T(128)S(1)} %broadcast_multiply_fusion.2), kind=kLoop, calls=%fused_computation.24.clone.1 | loop fusion | flops 524288 | bytes 4718608 | tf_op jit(solution)/shard_map/while/body/cos | solution.py:22
  231.4 4.3 mul.315
  235.7 11.5 %mul.316 = f32[4,16,64,512]{3,2,1,0:T(8,128)} reshape(f32[4,512,2,2,256]{4,3,2,1,0:T(2,128)} %mul.315) | data formatting | bytes 16777216 | tf_op jit(solution)/shard_map/while/body/mul | solution.py:30
  247.2 4.1 mul.317
  251.3 11.5 %mul.318 = f32[4,16,64,512]{3,2,1,0:T(8,128)} reshape(f32[4,512,2,2,256]{4,3,2,1,0:T(2,128)} %mul.317) | data formatting | bytes 16777216 | tf_op jit(solution)/shard_map/while/body/mul | solution.py:30
  267.4 2.9 squeeze.32
  278.8 11.5 %multiply_convert_fusion.3 = (bf16[4,16,64,512]{3,2,1,0:T(8,128)(2,1)}, bf16[4,16,64,512]{3,2,1,0:T(8,128)(2,1)}) fusion(f32[4,16,64,512]{3,2,1,0:T(8,128)} %mul.316, f32[4,16,64,512]{3,2,1,0:T(8,128)} %mul.318, f32[512]{0:T(512)S(1)} %bitcast.103, f32[16,64,512]{2,1,0:T(8,128)} %mul.319, f32[16,64,512]{2,1,0:T(8,128)} %mul.320), kind=kLoop, calls=%fused_computation.4.clone.1 | loop fusion | flops 20971520 | bytes 29362176 | tf_op jit(solution)/shard_map/while/body/convert_element_type | solution.py:35
  290.3 6.0 gather_fusion.1
  296.2 6.0 gather_fusion.3
  302.2 6.5 fusion.49
  308.7 6.1 gather_fusion
  314.8 6.1 gather_fusion.2
  320.9 5.8 add_bitcast_fusion.2
  330.0 3.9 subtract_bitcast_fusion.2
  333.8 5.4 maximum_add_fusion.2
  340.4 7.3 %multiply_cosine_fusion.2 = (f32[4,512,256]{2,1,0:T(8,128)S(1)}, f32[4,512,256]{2,1,0:T(8,128)S(1)}) fusion(f32[512,256]{1,0:T(8,128)S(1)} %multiply_add_fusion.2, f32[4]{0:T(128)S(1)} %broadcast_multiply_fusion.2), kind=kLoop, calls=%fused_computation.24.clone.1 | loop fusion | flops 524288 | bytes 4718608 | tf_op jit(solution)/shard_map/while/body/cos | solution.py:22
  347.6 4.3 mul.315
  352.0 11.5 %mul.316 = f32[4,16,64,512]{3,2,1,0:T(8,128)} reshape(f32[4,512,2,2,256]{4,3,2,1,0:T(2,128)} %mul.315) | data formatting | bytes 16777216 | tf_op jit(solution)/shard_map/while/body/mul | solution.py:30
  363.5 4.1 mul.317
  367.6 11.5 %mul.318 = f32[4,16,64,512]{3,2,1,0:T(8,128)} reshape(f32[4,512,2,2,256]{4,3,2,1,0:T(2,128)} %mul.317) | data formatting | bytes 16777216 | tf_op jit(solution)/shard_map/while/body/mul | solution.py:30
  395.0 11.5 %multiply_convert_fusion.3 = (bf16[4,16,64,512]{3,2,1,0:T(8,128)(2,1)}, bf16[4,16,64,512]{3,2,1,0:T(8,128)(2,1)}) fusion(f32[4,16,64,512]{3,2,1,0:T(8,128)} %mul.316, f32[4,16,64,512]{3,2,1,0:T(8,128)} %mul.318, f32[512]{0:T(512)S(1)} %bitcast.103, f32[16,64,512]{2,1,0:T(8,128)} %mul.319, f32[16,64,512]{2,1,0:T(8,128)} %mul.320), kind=kLoop, calls=%fused_computation.4.clone.1 | loop fusion | flops 20971520 | bytes 29362176 | tf_op jit(solution)/shard_map/while/body/convert_element_type | solution.py:35
  406.6 6.0 gather_fusion.1
  412.5 6.0 gather_fusion.3
  418.5 6.5 fusion.49
  425.0 6.1 gather_fusion
  431.1 6.1 gather_fusion.2
  437.2 5.8 add_bitcast_fusion.2
  446.2 3.9 subtract_bitcast_fusion.2
  450.1 5.4 maximum_add_fusion.2
  456.6 7.3 %multiply_cosine_fusion.2 = (f32[4,512,256]{2,1,0:T(8,128)S(1)}, f32[4,512,256]{2,1,0:T(8,128)S(1)}) fusion(f32[512,256]{1,0:T(8,128)S(1)} %multiply_add_fusion.2, f32[4]{0:T(128)S(1)} %broadcast_multiply_fusion.2), kind=kLoop, calls=%fused_computation.24.clone.1 | loop fusion | flops 524288 | bytes 4718608 | tf_op jit(solution)/shard_map/while/body/cos | solution.py:22
  463.9 4.3 mul.315
  468.3 11.5 %mul.316 = f32[4,16,64,512]{3,2,1,0:T(8,128)} reshape(f32[4,512,2,2,256]{4,3,2,1,0:T(2,128)} %mul.315) | data formatting | bytes 16777216 | tf_op jit(solution)/shard_map/while/body/mul | solution.py:30
  479.7 4.1 mul.317
  483.9 11.5 %mul.318 = f32[4,16,64,512]{3,2,1,0:T(8,128)} reshape(f32[4,512,2,2,256]{4,3,2,1,0:T(2,128)} %mul.317) | data formatting | bytes 16777216 | tf_op jit(solution)/shard_map/while/body/mul | solution.py:30
  511.3 11.5 %multiply_convert_fusion.3 = (bf16[4,16,64,512]{3,2,1,0:T(8,128)(2,1)}, bf16[4,16,64,512]{3,2,1,0:T(8,128)(2,1)}) fusion(f32[4,16,64,512]{3,2,1,0:T(8,128)} %mul.316, f32[4,16,64,512]{3,2,1,0:T(8,128)} %mul.318, f32[512]{0:T(512)S(1)} %bitcast.103, f32[16,64,512]{2,1,0:T(8,128)} %mul.319, f32[16,64,512]{2,1,0:T(8,128)} %mul.320), kind=kLoop, calls=%fused_computation.4.clone.1 | loop fusion | flops 20971520 | bytes 29362176 | tf_op jit(solution)/shard_map/while/body/convert_element_type | solution.py:35
  522.8 6.0 gather_fusion.1
  528.8 6.0 gather_fusion.3
  534.8 6.5 fusion.49
  541.3 6.1 gather_fusion
  547.4 6.1 gather_fusion.2
  553.5 5.8 add_bitcast_fusion.2
  562.5 3.9 subtract_bitcast_fusion.2
  566.4 5.4 maximum_add_fusion.2
  571.8 5.0 copy.12
  576.7 5.0 reshape.182
  581.7 74.7 %reduce-scatter.2.cloned.1.call-done = f32[17,2048]{1,0:T(8,128)} async-done(((f32[17,32768]{1,0:T(8,128)}), f32[17,2048]{1,0:T(8,128)}) %reduce-scatter.2.cloned.1.call-update) | async-done | bytes 139280 | tf_op jit(solution)/shard_map/reduce_scatter | solution.py:81
  (117 shorter events, 79.4 us)
Async XLA Ops:
  6.5 100.1 %copy-start.2 = (f32[3,512]{1,0:T(4,128)S(1)}, f32[3,512]{1,0:T(4,128)}, u32[]{:S(2)}) copy-start(f32[3,512]{1,0:T(4,128)} %param.15) | copy-start | bytes 18436
  6.5 100.1 %copy-start.3 = (f32[4]{0:T(128)S(1)}, f32[4]{0:T(128)}, u32[]{:S(2)}) copy-start(f32[4]{0:T(128)} %param.16) | copy-start | bytes 52
  6.5 97.5 %all-gather.2.cloned.1.call-start = ((), (), s32[]{:S(2)}) async-start(), calls=%async_computation.1 | async-start | bytes 9437184 | tf_op jit(solution)/shard_map/all_gather | solution.py:40
  9.5 646.9 %reduce-scatter.2.cloned.1.call-start = ((), (), s32[]{:S(2)}) async-start(), calls=%async_computation.2 | async-start | bytes 3342336 | tf_op jit(solution)/shard_map/reduce_scatter | solution.py:81
  198.5 11.9 %slice-start = ((s8[4456448]{0:T(1024)(128)(4,1)}), s8[262144]{0:T(1024)(128)(4,1)S(1)}, s32[]{:S(2)}) async-start(s8[4456448]{0:T(1024)(128)(4,1)} %bitcast.98), calls=%async_computation.3 | async-start | bytes 524288 | tf_op jit(solution)/shard_map/while
  204.6 5.8 slice-start.1
  204.6 6.8 %copy-start.1 = (bf16[17,4,64,512]{3,2,1,0:T(8,128)(2,1)S(1)}, bf16[17,4,64,512]{3,2,1,0:T(8,128)(2,1)}, u32[]{:S(2)}) copy-start(bf16[17,4,64,512]{3,2,1,0:T(8,128)(2,1)} %gather_fusion) | copy-start | bytes 13369348 | tf_op jit(solution)/shard_map/while
  211.4 2.3 copy-start
  314.8 11.9 %slice-start = ((s8[4456448]{0:T(1024)(128)(4,1)}), s8[262144]{0:T(1024)(128)(4,1)S(1)}, s32[]{:S(2)}) async-start(s8[4456448]{0:T(1024)(128)(4,1)} %bitcast.98), calls=%async_computation.3 | async-start | bytes 524288 | tf_op jit(solution)/shard_map/while
  320.9 5.8 slice-start.1
  320.9 6.8 %copy-start.1 = (bf16[17,4,64,512]{3,2,1,0:T(8,128)(2,1)S(1)}, bf16[17,4,64,512]{3,2,1,0:T(8,128)(2,1)}, u32[]{:S(2)}) copy-start(bf16[17,4,64,512]{3,2,1,0:T(8,128)(2,1)} %gather_fusion) | copy-start | bytes 13369348 | tf_op jit(solution)/shard_map/while
  327.7 2.3 copy-start
  431.1 11.9 %slice-start = ((s8[4456448]{0:T(1024)(128)(4,1)}), s8[262144]{0:T(1024)(128)(4,1)S(1)}, s32[]{:S(2)}) async-start(s8[4456448]{0:T(1024)(128)(4,1)} %bitcast.98), calls=%async_computation.3 | async-start | bytes 524288 | tf_op jit(solution)/shard_map/while
  437.2 5.8 slice-start.1
  437.2 6.8 %copy-start.1 = (bf16[17,4,64,512]{3,2,1,0:T(8,128)(2,1)S(1)}, bf16[17,4,64,512]{3,2,1,0:T(8,128)(2,1)}, u32[]{:S(2)}) copy-start(bf16[17,4,64,512]{3,2,1,0:T(8,128)(2,1)} %gather_fusion) | copy-start | bytes 13369348 | tf_op jit(solution)/shard_map/while
  444.0 2.3 copy-start
  547.4 11.9 %slice-start = ((s8[4456448]{0:T(1024)(128)(4,1)}), s8[262144]{0:T(1024)(128)(4,1)S(1)}, s32[]{:S(2)}) async-start(s8[4456448]{0:T(1024)(128)(4,1)} %bitcast.98), calls=%async_computation.3 | async-start | bytes 524288 | tf_op jit(solution)/shard_map/while
  553.5 5.8 slice-start.1
  553.5 6.8 %copy-start.1 = (bf16[17,4,64,512]{3,2,1,0:T(8,128)(2,1)S(1)}, bf16[17,4,64,512]{3,2,1,0:T(8,128)(2,1)}, u32[]{:S(2)}) copy-start(bf16[17,4,64,512]{3,2,1,0:T(8,128)(2,1)} %gather_fusion) | copy-start | bytes 13369348 | tf_op jit(solution)/shard_map/while
  560.3 2.3 copy-start
Sparse Core Ops, SparseCore 0:
  9.6 94.3 all-gather.1
  581.8 74.5 reduce-scatter.1
where the time goes:
time: 667 us; the launch traced here: 663 us
  local copies, waits for them, and re-layouts  301 us (45%)
  waiting for transfers between devices  167 us (25%)
  other arithmetic  110 us (16%)
  matrix products  70.6 us (11%)
  between operations  14.1 us (2%)
    mul x24, local copies, waits for them, and re-layouts, beam_field(): field_re = (real_jones * cosine + imag_jones * sine_part) * amplitude  148 us
    all_gather x1, waiting for transfers between devices, gather_beams(): return lax.all_gather(jones_part, 'stn', axis=1, tiled=True)  92.4 us
    reduce_scatter x1, waiting for transfers between devices, body(): lax.psum_scatter(totals.reshape(local_pairs, -1), 'src', scatter_dimensio...  74.7 us
    dot_general x16, matrix products, gram(): jnp.einsum('cnxk,cnyk->ncxy', left, right, preferred_element_type=jnp.flo...  70.6 us
    convert_element_type x4, other arithmetic, beam_field(): field_im.reshape(out_shape).astype(jnp.bfloat16)  46 us
    cos x4, other arithmetic, beam_field(): cosine = jnp.cos(phases)[:, :, None, None, :]  29.2 us
    gather x4, local copies, waits for them, and re-layouts, one_turn(): right_re = jnp.take(field_re, right_block, axis=1)  24.4 us
    gather x4, local copies, waits for them, and re-layouts, one_turn(): left_re = jnp.take(field_re, left_block, axis=1)  24.4 us
  transfers between devices with their start and end apart: 2, of which 2 were waited for; matrix products, arithmetic and copies ran while one was open for 0% of the time, Pallas kernels for 0%

commit v1 on v0

v1 whole, which is shorter than its diff:
```python
import functools
import math

import jax
import jax.numpy as jnp
import numpy as np
from jax import lax
from jax.experimental import pallas as pl
from jax.experimental.pallas import tpu as pltpu
from jax.sharding import PartitionSpec as P

NBLK = 16
STN = 8
PAIRS_DEV = 17
LANES = 128
JROWS = 512
EXTRA = 16
ROWS = JROWS + EXTRA
KCOL = 1024
SEND_SCALE = 1.0

TWO_PI_HI = 6.28125
TWO_PI_LO = 2.0 * math.pi - 6.28125
def _fit(fun, power, terms):
    x = np.cos(np.pi * (np.arange(4000) + 0.5) / 4000) * (math.pi * 1.001)
    cols = np.stack([x ** (2 * n + power) for n in range(terms)], 1)
    scale = np.abs(cols).max(0)
    sol, *_ = np.linalg.lstsq(cols / scale, fun(x), rcond=None)
    return [float(v) for v in sol / scale]


SIN_TERMS = _fit(np.sin, 1, 7)
COS_TERMS = _fit(np.cos, 0, 8)


def horner(square, terms):
    total = jnp.full_like(square, terms[-1])
    for term in terms[-2::-1]:
        total = total * square + term
    return total


def three(rows, at):
    return (rows[at : at + 1] + rows[at + 1 : at + 2]) + rows[at + 2 : at + 3]


def field_slab(pieces, uvw_ref, scale, kappa, g_ref, l_ref):
    for h, parts in enumerate(pieces):
        info = parts[0][0][0, JROWS:ROWS, :].astype(jnp.float32)
        dir_l, dir_m, depth, amp = (three(info, 3 * n) for n in range(4))
        for ref, first in parts:
            count = ref.shape[0]

            def step(at, carry, ref=ref, first=first):
                blk = 2 * first + at
                row = pl.multiple_of(32 * (at % 2), 32)
                here = pl.ds(pl.multiple_of(32 * blk, 32), 32)
                geometry = (
                    uvw_ref[0, here, :] * dir_l + uvw_ref[1, here, :] * dir_m
                ) + uvw_ref[2, here, :] * depth
                phase = scale * geometry
                turns = jnp.round(phase * (0.5 / math.pi))
                angle = (phase - turns * TWO_PI_HI) - turns * TWO_PI_LO
                square = angle * angle
                sine = horner(square, SIN_TERMS) * (angle * amp)
                cosine = horner(square, COS_TERMS) * amp
                for a in range(2):
                    g_rows = pl.ds(pl.multiple_of(64 * blk + 32 * a, 32), 32)
                    own = pl.ds(pl.multiple_of(64 * blk + 32 * a + 16 * kappa, 16), 16)
                    l_re = pl.ds(pl.multiple_of(32 * blk + 16 * a, 16), 16)
                    l_im = pl.ds(pl.multiple_of(512 + 32 * blk + 16 * a, 16), 16)
                    for k in range(2):
                        comp = 2 * a + k
                        real = ref[at // 2, pl.ds(64 * comp + row, 32), :].astype(jnp.float32)
                        imag = ref[at // 2, pl.ds(64 * (4 + comp) + row, 32), :].astype(jnp.float32)
                        c_re = slice((4 * h + 2 * k) * LANES, (4 * h + 2 * k + 1) * LANES)
                        c_im = slice((4 * h + 2 * k + 1) * LANES, (4 * h + 2 * k + 2) * LANES)
                        g_ref[g_rows, c_re] = (real * cosine + imag * sine).astype(jnp.bfloat16)
                        g_ref[g_rows, c_im] = (imag * cosine - real * sine).astype(jnp.bfloat16)
                        x_re = g_ref[own, c_re]
                        x_im = g_ref[own, c_im]
                        l_ref[l_re, c_re] = x_re
                        l_ref[l_re, c_im] = x_im
                        l_ref[l_im, c_re] = x_im
                        l_ref[l_im, c_im] = -x_re
                return carry

            lax.fori_loop(0, 2 * count, step, 0)


def gram_slab(l_ref, g_ref, acc_ref, add):
    for tile in range(4):
        rows = (tile + 1) * 128
        cols = slice(256 * tile, 256 * tile + 256)
        for part in range(2):
            at = slice(512 * part, 512 * part + rows)
            got = lax.dot_general(
                l_ref[at, :], g_ref[cols, :], (((1,), (1,)), ((), ())),
                preferred_element_type=jnp.float32,
            )
            acc_ref[at, cols] = (acc_ref[at, cols] + got) if add else got


def near_kernel(slabs, scal_ref, kap_ref, uvw_ref, *refs):
    acc_ref, g_ref, l_ref = refs[-3:]
    for n in range(slabs):
        pieces = [[(refs[2 * n], 0)], [(refs[2 * n + 1], 0)]]
        field_slab(pieces, uvw_ref, scal_ref[0], kap_ref[0], g_ref, l_ref)
        gram_slab(l_ref, g_ref, acc_ref, n > 0)


def far_kernel(scal_ref, kap_ref, idx_ref, uvw_ref, a0, b0, a1, b1, near_ref, out_ref, acc_ref, g_ref, l_ref):
    pieces = [[(a0, 0), (b0, 4)], [(a1, 0), (b1, 4)]]
    field_slab(pieces, uvw_ref, scal_ref[0], kap_ref[0], g_ref, l_ref)
    gram_slab(l_ref, g_ref, acc_ref, False)
    low = lax.broadcasted_iota(jnp.int32, (16, LANES), 1) < 64
    for i in range(NBLK):
        for tile in range(i // 2, NBLK // 2):
            cols = slice(LANES * tile, LANES * tile + LANES)
            for part in range(2):
                top = 512 * part + 32 * i
                row0 = (acc_ref[top : top + 16, cols] + near_ref[top : top + 16, cols]) * SEND_SCALE
                row1 = (acc_ref[top + 16 : top + 32, cols] + near_ref[top + 16 : top + 32, cols]) * SEND_SCALE
                if i <= 2 * tile:
                    even = jnp.where(low, row0, pltpu.roll(row1, 64, 1))
                    out_ref[idx_ref[i * NBLK + 2 * tile] + PAIRS_DEV * part] = even.astype(out_ref.dtype)
                odd = jnp.where(low, pltpu.roll(row0, 64, 1), row1)
                out_ref[idx_ref[i * NBLK + 2 * tile + 1] + PAIRS_DEV * part] = odd.astype(out_ref.dtype)


def sum_kernel(got_ref, order_ref, out_ref, held_ref):
    total = got_ref[0].astype(jnp.float32)
    for n in range(1, got_ref.shape[0]):
        total = total + got_ref[n].astype(jnp.float32)
    total = total * (1.0 / SEND_SCALE)
    held_ref[...] = jnp.dot(
        total, order_ref[...], precision=lax.Precision.HIGHEST, preferred_element_type=jnp.float32
    )
    for st in range(16):
        out_ref[:, LANES * st : LANES * st + LANES] = held_ref[pl.ds(st, PAIRS_DEV, stride=16), :]


VMEM = pl.BlockSpec(memory_space=pltpu.VMEM)
SMEM = pl.BlockSpec(memory_space=pltpu.SMEM)
PARAMS = pltpu.CompilerParams(vmem_limit_bytes=56 * 1024 * 1024)
WORK = [pltpu.VMEM((KCOL, KCOL), jnp.bfloat16), pltpu.VMEM((KCOL, KCOL), jnp.bfloat16)]
SEND = jnp.bfloat16


def src_step(dz, dcore):
    return [
        (z * 4 + xh * 2 + core, ((z + dz) % 4) * 4 + xh * 2 + (core ^ dcore))
        for z in range(4) for xh in range(2) for core in range(2)
    ]


PLANES = [
    [stn * 16 + z * 4 + xh * 2 + core for stn in range(STN) for xh in range(2)]
    for z in range(4) for core in range(2)
]


def split3(x):
    first = lax.reduce_precision(x, 8, 7)
    second = lax.reduce_precision(x - first, 8, 7)
    third = x - first - second
    return [v.astype(jnp.bfloat16) for v in (first, second, third)]


def body(beam_jones, source_lm, source_flux, live_counts, station_uvw, chan_scale, block_pairs):
    src = lax.axis_index("src")
    plane = src // 4
    kappa = (src % 2).astype(jnp.int32).reshape(1)
    slots = beam_jones.shape[2]
    live = (jnp.arange(slots, dtype=jnp.int32) < live_counts[0]).astype(jnp.float32)
    amp = jnp.sqrt(source_flux * live / math.sqrt(slots * 16))
    dir_l, dir_m = source_lm[0], source_lm[1]
    depth = jnp.sqrt(1.0 - dir_l * dir_l - dir_m * dir_m) - 1.0
    extra = []
    for row in (dir_l, dir_m, depth, amp):
        extra += [v.reshape(STN, LANES) for v in split3(row)]
    pairs = jnp.pad(block_pairs.T.astype(jnp.bfloat16), ((0, 0), (0, LANES - PAIRS_DEV)))
    extra += [jnp.broadcast_to(pairs[n][None], (STN, LANES)) for n in range(2)]
    extra += [jnp.zeros((STN, LANES), jnp.bfloat16)] * (EXTRA - len(extra))
    extra = jnp.stack(extra, axis=1)
    pieces = jnp.transpose(beam_jones.reshape(JROWS, STN, LANES), (1, 0, 2))
    message = jnp.concatenate([pieces, extra], axis=1)

    own = lax.all_to_all(message, "stn", 0, 0, tiled=True)

    def move(x, dz, dcore=0):
        return lax.ppermute(x, "src", src_step(dz, dcore))

    below = move(own, 1)
    above = move(own, -1)
    far_a = move(below[:4], 1)
    far_b = move(above[4:], -1)
    near = []
    for slab in (own, below, above):
        near += [slab, move(slab, 0, 1)]
    far = [far_a, far_b, move(far_a, 0, 1), move(far_b, 0, 1)]

    listed = own[:, JROWS + 12 : JROWS + 14, :PAIRS_DEV].astype(jnp.int32)
    number = jnp.arange(STN * PAIRS_DEV, dtype=jnp.int32)
    place = (number // PAIRS_DEV) * (2 * PAIRS_DEV) + number % PAIRS_DEV
    key = (listed[:, 0] * NBLK + listed[:, 1]).reshape(1, -1)
    hit = key == jnp.arange(NBLK * NBLK, dtype=jnp.int32)[:, None]
    index = jnp.sum(jnp.where(hit, place[None], 0), axis=1)

    scale = (2.0 * math.pi * chan_scale)[plane].reshape(1)
    uvw = jnp.broadcast_to(station_uvw[:, :, None], (3, station_uvw.shape[1], LANES))

    partial = pl.pallas_call(
        functools.partial(near_kernel, 3),
        out_shape=jax.ShapeDtypeStruct((KCOL, KCOL), jnp.float32),
        in_specs=[SMEM, SMEM, VMEM] + [VMEM] * 6,
        out_specs=VMEM,
        scratch_shapes=WORK,
        compiler_params=PARAMS,
        cost_estimate=pl.CostEstimate(flops=4_000_000_000, bytes_accessed=11_000_000, transcendentals=0),
    )(scale, kappa, uvw, *near)
    send = pl.pallas_call(
        far_kernel,
        out_shape=jax.ShapeDtypeStruct((STN * 2 * PAIRS_DEV, 16, LANES), SEND),
        in_specs=[SMEM, SMEM, SMEM, VMEM] + [VMEM] * 5,
        out_specs=VMEM,
        scratch_shapes=[pltpu.VMEM((KCOL, KCOL), jnp.float32)] + WORK,
        compiler_params=PARAMS,
        cost_estimate=pl.CostEstimate(flops=1_400_000_000, bytes_accessed=8_000_000, transcendentals=0),
    )(scale, kappa, index, uvw, *far, partial)

    send = send.reshape(STN * 2, PAIRS_DEV * 16, LANES)
    got = lax.all_to_all(send, ("stn", "src"), 0, 0, axis_index_groups=PLANES, tiled=True)

    lane = np.arange(LANES)
    order = np.zeros((LANES, LANES), np.float32)
    order[lane, (lane // 64) * 64 + (lane % 32) * 2 + (lane // 32) % 2] = 1.0
    return pl.pallas_call(
        sum_kernel,
        out_shape=jax.ShapeDtypeStruct((PAIRS_DEV, 2048), jnp.float32),
        in_specs=[VMEM, VMEM],
        out_specs=VMEM,
        scratch_shapes=[pltpu.VMEM((PAIRS_DEV * 16, LANES), jnp.float32)],
        compiler_params=PARAMS,
    )(got, jnp.asarray(order))


def solution(mesh):
    placed = (P(None, "stn", "src"), P(None, "src"), P("src"), P("src"), P(), P(), P("stn", None))
    return jax.shard_map(
        body, mesh=mesh, in_specs=placed, out_specs=P("stn", "src"), check_vma=False
    )
```

time: 667 us -> 129 us (0.19)
  local copies, waits for them, and re-layouts: 301 us -> 7.84 us
  waiting for transfers between devices: 167 us -> 33.7 us
  other arithmetic: 110 us -> 2.94 us
  matrix products: 70.6 us -> 0 us
  blocking collectives: 0 us -> 46 us
  Pallas kernels: 0 us -> 28.6 us
  between operations: 14.1 us -> 0.79 us
  starting transfers between devices: 0.04 us -> 7.93 us
    mul x24 -> x0, local copies, waits for them, and re-layouts: 148 us -> none  [beam_field(): field_re = (real_jones * cosine + imag_jones * sine_part) * amplitude]
    gather x16 -> x0, local copies, waits for them, and re-layouts: 96.5 us -> none  [the longest x4 24.4 us: one_turn(): right_re = jnp.take(field_re, right_block, axis=1)]
    all_gather x1 -> x0, waiting for transfers between devices: 92.4 us -> none  [gather_beams(): return lax.all_gather(jones_part, 'stn', axis=1, tiled=True)]
    reduce_scatter x1 -> x0, waiting for transfers between devices: 74.7 us -> none  [body(): lax.psum_scatter(totals.reshape(local_pairs, -1), 'src', scatter_dimensio...]
    dot_general x16 -> x0, matrix products: 70.6 us -> none  [gram(): jnp.einsum('cnxk,cnyk->ncxy', left, right, preferred_element_type=jnp.flo...]
    convert_element_type x8 -> x4, other arithmetic: 53.6 us -> 1.52 us  [the longest x2 0.83 us: split3(): return [v.astype(jnp.bfloat16) for v in (first, second, third)]]
    all_to_all x0 -> x2, blocking collectives: none -> 46 us  [the longest x1 24.3 us: body(): lax.all_to_all(send, ('stn', 'src'), 0, 0, axis_index_groups=PLANES, tile...]
    ppermute x0 -> x9, waiting for transfers between devices: none -> 33.7 us  [move(): return lax.ppermute(x, 'src', src_step(dz, dcore))]
  transfers between devices with their start and end apart: 2 -> 9, of which waited for: 2 -> 3; matrix products, arithmetic and copies ran while one was open for 0% -> 4% of each run, Pallas kernels for 0% -> 14%
where the time goes in v1:
time: 129 us; the launch traced here: 128 us
  blocking collectives  46 us (36%)
  waiting for transfers between devices  33.7 us (26%)
  Pallas kernels  28.6 us (22%)
  starting transfers between devices  7.93 us (6%)
  local copies, waits for them, and re-layouts  7.84 us (6%)
  other arithmetic  2.94 us (2%)
    ppermute x9, waiting for transfers between devices, move(): return lax.ppermute(x, 'src', src_step(dz, dcore))  33.7 us
    all_to_all x1, blocking collectives, body(): lax.all_to_all(send, ('stn', 'src'), 0, 0, axis_index_groups=PLANES, tile...  24.3 us
    all_to_all x1, blocking collectives, body(): own = lax.all_to_all(message, 'stn', 0, 0, tiled=True)  21.7 us
    pallas_call x1, Pallas kernels, body(): pl.pallas_call(functools.partial(near_kernel, 3), out_shape=jax.ShapeDtyp...  17.4 us
    pallas_call x1, Pallas kernels, body(): pl.pallas_call(far_kernel, out_shape=jax.ShapeDtypeStruct((STN * 2 * PAIR...  8.85 us
    ppermute x9, starting transfers between devices, move(): return lax.ppermute(x, 'src', src_step(dz, dcore))  7.93 us
    unnamed x15, local copies, waits for them, and re-layouts  3.14 us
  transfers between devices with their start and end apart: 9, of which 3 were waited for; matrix products, arithmetic and copies ran while one was open for 4% of the time, Pallas kernels for 14%

profile of v1, /device:TPU:0, one launch (start us, length us, event | category | flops | bytes accessed | tf_op | source)
XLA Modules:
  0.0 127.7 jit_solution(11158005080711341319)
XLA Ops:
  0.0 0.8 fusion.2
  1.5 0.7 fusion.7
  2.2 0.7 convert_bitcast_fusion
  2.9 1.5 %copy.22 = bf16[64,8,8,128]{3,2,1,0:T(8,128)(2,1)S(1)} copy(bf16[64,8,8,128]{3,1,2,0:T(8,128)(2,1)} %bitcast.54) | data formatting | bytes 2097152
  4.4 0.1 copy.24
  4.6 0.5 concatenate.7
  5.1 21.7 %all_to_all.10.refs_0_ = bf16[8,528,128]{2,1,0:T(8,128)(2,1)S(1)} all-to-all(bf16[8,528,128]{2,1,0:T(8,128)(2,1)S(1)} %concatenate.7), channel_id=1, replica_groups=mesh['stn'=8,'src'=16] {'stn'}, dimensions={0} | all-to-all | bytes 2162688 | tf_op jit(solution)/shard_map/all_to_all | solution.py:189
  26.7 0.0 copy-start
  26.7 1.9 %collective-permute-start = (bf16[8,528,128]{2,1,0:T(8,128)(2,1)S(1)}, bf16[8,528,128]{2,1,0:T(8,128)(2,1)}, u32[]{:S(2)}, u32[]{:S(2)}) collective-permute-start(bf16[8,528,128]{2,1,0:T(8,128)(2,1)S(1)} %all_to_all.10.refs_0_), channel_id=1, source_target_pairs={{0,4},{1,5},{2,6},{3,7},{4,8},{5,9},{6,10},{7,11},{8,12},{9,13},{1... | collective-permute-start | bytes 3244040 | tf_op jit(solution)/shard_map/ppermute | solution.py:192
  28.7 2.1 %collective-permute-start.2 = (bf16[8,528,128]{2,1,0:T(8,128)(2,1)S(1)}, bf16[8,528,128]{2,1,0:T(8,128)(2,1)}, u32[]{:S(2)}, u32[]{:S(2)}) collective-permute-start(bf16[8,528,128]{2,1,0:T(8,128)(2,1)S(1)} %all_to_all.10.refs_0_), channel_id=1, source_target_pairs={{0,12},{1,13},{2,14},{3,15},{4,0},{5,1},{6,2},{7,3},{8,4},{9,5},{1... | collective-permute-start | bytes 3244040 | tf_op jit(solution)/shard_map/ppermute | solution.py:192
  30.8 0.0 collective-permute-start.6
  30.8 22.4 %collective-permute-done.refs_2_ = bf16[8,528,128]{2,1,0:T(8,128)(2,1)} collective-permute-done((bf16[8,528,128]{2,1,0:T(8,128)(2,1)S(1)}, bf16[8,528,128]{2,1,0:T(8,128)(2,1)}, u32[]{:S(2)}, u32[]{:S(2)}) %collective-permute-start) | collective-permute-done | bytes 1081376 | tf_op jit(solution)/shard_map/ppermute | solution.py:192
  53.2 0.0 collective-permute-start.7
  53.2 0.0 collective-permute-done.2.refs_4_
  53.2 0.5 collective-permute-start.8
  53.7 0.0 copy-start.6
  53.7 0.0 copy-start.5
  53.7 1.1 slice.45
  54.8 0.8 collective-permute-start.1
  55.6 1.1 slice.46
  56.7 2.6 %collective-permute-start.3 = (bf16[4,528,128]{2,1,0:T(8,128)(2,1)S(1)}, bf16[4,528,128]{2,1,0:T(8,128)(2,1)S(1)}, u32[]{:S(2)}, u32[]{:S(2)}) collective-permute-start(bf16[4,528,128]{2,1,0:T(8,128)(2,1)S(1)} %slice.46), channel_id=1, source_target_pairs={{0,12},{1,13},{2,14},{3,15},{4,0},{5,1},{6,2},{7,3},{8,4},{9,5},{1... | collective-permute-start | bytes 1622024 | tf_op jit(solution)/shard_map/ppermute | solution.py:192
  59.3 0.0 copy-done.6
  59.3 0.6 dynamic_slice.3.scal_ref
  59.9 0.0 copy-done
  59.9 10.3 %collective-permute-done.1.a0 = bf16[4,528,128]{2,1,0:T(8,128)(2,1)S(1)} collective-permute-done((bf16[4,528,128]{2,1,0:T(8,128)(2,1)S(1)}, bf16[4,528,128]{2,1,0:T(8,128)(2,1)S(1)}, u32[]{:S(2)}, u32[]{:S(2)}) %collective-permute-start.1) | collective-permute-done | bytes 540704 | tf_op jit(solution)/shard_map/ppermute | solution.py:192
  70.3 0.0 copy-start.1
  70.3 0.0 collective-permute-start.4
  70.3 0.9 collective-permute-done.3.b0
  71.2 0.0 copy-start.2
  71.2 0.0 collective-permute-start.5
  71.2 0.1 add.61
  71.3 0.7 select_reduce_fusion.idx_ref
  72.0 0.0 collective-permute-done.6.refs_1_
  72.0 0.0 collective-permute-done.7.refs_3_
  72.0 0.0 collective-permute-done.8.refs_5_
  72.0 0.0 copy-done.5
  72.0 1.2 broadcast_in_dim.22.uvw_ref
  73.2 17.4 %shard_map.82.near_ref = f32[1024,1024]{1,0:T(8,128)} custom-call(f32[1]{0:T(128)} %dynamic_slice.3.scal_ref, s32[1]{0:T(128)} %bitcast.kap_ref, f32[3,512,128]{2,1,0:T(8,128)} %broadcast_in_dim.22.uvw_ref, bf16[8,528,128]{2,1,0:T(8,128)(2,1)} %copy-done, bf16[8,528,128]{2,1,0:T(8,128)(2,1)} %collective-permute-done.6.refs_1_, ...), custom_call_target="tpu_custom_call" | custom-call | flops 4000000000 | bytes 11000000 | tf_op jit(solution)/shard_map/pallas_call | solution.py:213
  90.6 0.0 copy-done.1
  90.6 0.0 copy-done.2
  90.6 0.0 collective-permute-done.4.a1
  90.6 0.0 copy-start.3
  90.6 0.0 collective-permute-done.5.b1
  90.6 0.8 copy-done.3
  91.4 0.0 copy-start.4
  91.5 0.8 copy-done.4
  92.3 8.8 %shard_map.83 = bf16[272,16,128]{2,1,0:T(8,128)(2,1)} custom-call(f32[1]{0:T(128)} %dynamic_slice.3.scal_ref, s32[1]{0:T(128)} %bitcast.kap_ref, s32[256]{0:T(256)} %select_reduce_fusion.idx_ref, f32[3,512,128]{2,1,0:T(8,128)} %broadcast_in_dim.22.uvw_ref, bf16[4,528,128]{2,1,0:T(8,128)(2,1)} %copy-done.1, bf16[4,528,128]{2,1,0:T(8,128)(2,1)} %copy-done.2, ...), custom_call_target="tpu_custom_call" | custom-call | flops 1400000000 | bytes 8000000 | tf_op jit(solution)/shard_map/pallas_call | solution.py:222
  101.1 24.3 %all_to_all.11.got_ref = bf16[16,272,128]{2,1,0:T(8,128)(2,1)} all-to-all(bf16[16,272,128]{2,1,0:T(8,128)(2,1)} %bitcast.51), channel_id=1, replica_groups={{0,2,16,18,32,34,48,50,64,66,80,82,96,98,112,114},{1,3,17,19,33,35,49,5..., dimensions={0} | all-to-all | bytes 2228224 | tf_op jit(solution)/shard_map/all_to_all | solution.py:233
  125.4 2.3 %shard_map.84 = f32[17,2048]{1,0:T(8,128)} custom-call(bf16[16,272,128]{2,1,0:T(8,128)(2,1)} %all_to_all.11.got_ref, f32[128,128]{1,0:T(8,128)} %constant.69.clone.order_ref), custom_call_target="tpu_custom_call" | custom-call | tf_op jit(solution)/shard_map/pallas_call | solution.py:238
  (13 shorter events, 0.1 us)
Async XLA Ops:
  26.7 33.2 %copy-start = (bf16[8,528,128]{2,1,0:T(8,128)(2,1)}, bf16[8,528,128]{2,1,0:T(8,128)(2,1)S(1)}, u32[]{:S(2)}) copy-start(bf16[8,528,128]{2,1,0:T(8,128)(2,1)S(1)} %all_to_all.10.refs_0_) | copy-start | bytes 3244036
  26.7 26.4 %collective-permute-start = (bf16[8,528,128]{2,1,0:T(8,128)(2,1)S(1)}, bf16[8,528,128]{2,1,0:T(8,128)(2,1)}, u32[]{:S(2)}, u32[]{:S(2)}) collective-permute-start(bf16[8,528,128]{2,1,0:T(8,128)(2,1)S(1)} %all_to_all.10.refs_0_), channel_id=1, source_target_pairs={{0,4},{1,5},{2,6},{3,7},{4,8},{5,9},{6,10},{7,11},{8,12},{9,13},{1... | collective-permute-start | bytes 3244040 | tf_op jit(solution)/shard_map/ppermute | solution.py:192
  28.7 24.5 %collective-permute-start.2 = (bf16[8,528,128]{2,1,0:T(8,128)(2,1)S(1)}, bf16[8,528,128]{2,1,0:T(8,128)(2,1)}, u32[]{:S(2)}, u32[]{:S(2)}) collective-permute-start(bf16[8,528,128]{2,1,0:T(8,128)(2,1)S(1)} %all_to_all.10.refs_0_), channel_id=1, source_target_pairs={{0,12},{1,13},{2,14},{3,15},{4,0},{5,1},{6,2},{7,3},{8,4},{9,5},{1... | collective-permute-start | bytes 3244040 | tf_op jit(solution)/shard_map/ppermute | solution.py:192
  30.8 41.2 %collective-permute-start.6 = (bf16[8,528,128]{2,1,0:T(8,128)(2,1)S(1)}, bf16[8,528,128]{2,1,0:T(8,128)(2,1)}, u32[]{:S(2)}, u32[]{:S(2)}) collective-permute-start(bf16[8,528,128]{2,1,0:T(8,128)(2,1)S(1)} %all_to_all.10.refs_0_), channel_id=1, source_target_pairs={{0,1},{1,0},{2,3},{3,2},{4,5},{5,4},{6,7},{7,6},{8,9},{9,8},{10,11... | collective-permute-start | bytes 3244040 | tf_op jit(solution)/shard_map/ppermute | solution.py:192
  53.2 18.8 %collective-permute-start.7 = (bf16[8,528,128]{2,1,0:T(8,128)(2,1)}, bf16[8,528,128]{2,1,0:T(8,128)(2,1)}, u32[]{:S(2)}, u32[]{:S(2)}) collective-permute-start(bf16[8,528,128]{2,1,0:T(8,128)(2,1)} %collective-permute-done.refs_2_), channel_id=1, source_target_pairs={{0,1},{1,0},{2,3},{3,2},{4,5},{5,4},{6,7},{7,6},{8,9},{9,8},{10,11... | collective-permute-start | bytes 3244040 | tf_op jit(solution)/shard_map/ppermute | solution.py:192
  53.2 18.8 %collective-permute-start.8 = (bf16[8,528,128]{2,1,0:T(8,128)(2,1)}, bf16[8,528,128]{2,1,0:T(8,128)(2,1)}, u32[]{:S(2)}, u32[]{:S(2)}) collective-permute-start(bf16[8,528,128]{2,1,0:T(8,128)(2,1)} %collective-permute-done.2.refs_4_), channel_id=1, source_target_pairs={{0,1},{1,0},{2,3},{3,2},{4,5},{5,4},{6,7},{7,6},{8,9},{9,8},{10,11... | collective-permute-start | bytes 3244040 | tf_op jit(solution)/shard_map/ppermute | solution.py:192
  53.7 5.6 %copy-start.6 = (f32[4]{0:T(128)S(1)}, f32[4]{0:T(128)}, u32[]{:S(2)}) copy-start(f32[4]{0:T(128)} %param.13) | copy-start | bytes 52
  53.7 18.3 %copy-start.5 = (f32[3,512]{1,0:T(4,128)S(1)}, f32[3,512]{1,0:T(4,128)}, u32[]{:S(2)}) copy-start(f32[3,512]{1,0:T(4,128)} %param.12) | copy-start | bytes 18436
  54.8 15.5 %collective-permute-start.1 = (bf16[4,528,128]{2,1,0:T(8,128)(2,1)S(1)}, bf16[4,528,128]{2,1,0:T(8,128)(2,1)S(1)}, u32[]{:S(2)}, u32[]{:S(2)}) collective-permute-start(bf16[4,528,128]{2,1,0:T(8,128)(2,1)S(1)} %slice.45), channel_id=1, source_target_pairs={{0,4},{1,5},{2,6},{3,7},{4,8},{5,9},{6,10},{7,11},{8,12},{9,13},{1... | collective-permute-start | bytes 1622024 | tf_op jit(solution)/shard_map/ppermute | solution.py:192
  56.7 14.5 %collective-permute-start.3 = (bf16[4,528,128]{2,1,0:T(8,128)(2,1)S(1)}, bf16[4,528,128]{2,1,0:T(8,128)(2,1)S(1)}, u32[]{:S(2)}, u32[]{:S(2)}) collective-permute-start(bf16[4,528,128]{2,1,0:T(8,128)(2,1)S(1)} %slice.46), channel_id=1, source_target_pairs={{0,12},{1,13},{2,14},{3,15},{4,0},{5,1},{6,2},{7,3},{8,4},{9,5},{1... | collective-permute-start | bytes 1622024 | tf_op jit(solution)/shard_map/ppermute | solution.py:192
  70.3 20.3 %copy-start.1 = (bf16[4,528,128]{2,1,0:T(8,128)(2,1)}, bf16[4,528,128]{2,1,0:T(8,128)(2,1)S(1)}, u32[]{:S(2)}) copy-start(bf16[4,528,128]{2,1,0:T(8,128)(2,1)S(1)} %collective-permute-done.1.a0) | copy-start | bytes 1622020
  70.3 20.3 %collective-permute-start.4 = (bf16[4,528,128]{2,1,0:T(8,128)(2,1)S(1)}, bf16[4,528,128]{2,1,0:T(8,128)(2,1)S(1)}, u32[]{:S(2)}, u32[]{:S(2)}) collective-permute-start(bf16[4,528,128]{2,1,0:T(8,128)(2,1)S(1)} %collective-permute-done.1.a0), channel_id=1, source_target_pairs={{0,1},{1,0},{2,3},{3,2},{4,5},{5,4},{6,7},{7,6},{8,9},{9,8},{10,11... | collective-permute-start | bytes 1622024 | tf_op jit(solution)/shard_map/ppermute | solution.py:192
  71.2 19.4 %copy-start.2 = (bf16[4,528,128]{2,1,0:T(8,128)(2,1)}, bf16[4,528,128]{2,1,0:T(8,128)(2,1)S(1)}, u32[]{:S(2)}) copy-start(bf16[4,528,128]{2,1,0:T(8,128)(2,1)S(1)} %collective-permute-done.3.b0) | copy-start | bytes 1622020
  71.2 19.4 %collective-permute-start.5 = (bf16[4,528,128]{2,1,0:T(8,128)(2,1)S(1)}, bf16[4,528,128]{2,1,0:T(8,128)(2,1)S(1)}, u32[]{:S(2)}, u32[]{:S(2)}) collective-permute-start(bf16[4,528,128]{2,1,0:T(8,128)(2,1)S(1)} %collective-permute-done.3.b0), channel_id=1, source_target_pairs={{0,1},{1,0},{2,3},{3,2},{4,5},{5,4},{6,7},{7,6},{8,9},{9,8},{10,11... | collective-permute-start | bytes 1622024 | tf_op jit(solution)/shard_map/ppermute | solution.py:192
  90.6 0.8 copy-start.3
  91.4 0.8 copy-start.4
